TPU v7x, 32 devices: a whole 2x2x4 slice. The times are simulated.
32 devices in a mesh: dp: 16 (over z, x, core), tensor: 2 (over y).
Axes of the slice: x: 2, y: 2, z: 4, core: 2. Of those that a mesh axis runs over, the one named last changes fastest.
Arguments:
- tokens: bfloat16 [2, 8192, 1152], P(None, 'dp'), may hold values from -6 to 6
- image_starts: int32 [2, 16], P(None, 'dp'), may hold values from 0 to 256
- g_attn_in: float32 [1152], replicated, may hold values from 0.5 to 1.5
- w_query: bfloat16 [1152, 1024], P(None, 'tensor'), may hold values from -0.1875 to 0.1875
- w_key: bfloat16 [1152, 256], replicated, may hold values from -0.1875 to 0.1875
- w_value: bfloat16 [1152, 256], replicated, may hold values from -0.1875 to 0.1875
- g_query: float32 [256], replicated, may hold values from 0.25 to 1.75
- g_key: float32 [256], replicated, may hold values from 0.25 to 1.75
- w_out: bfloat16 [1024, 1152], P('tensor'), may hold values from -0.1875 to 0.1875
- g_attn_post: float32 [1152], replicated, may hold values from 0.5 to 1.5
- g_ffn_in: float32 [1152], replicated, may hold values from 0.5 to 1.5
- w_gate: bfloat16 [1152, 6912], P(None, 'tensor'), may hold values from -0.1875 to 0.1875
- w_up: bfloat16 [1152, 6912], P(None, 'tensor'), may hold values from -0.1875 to 0.1875
- w_down: bfloat16 [6912, 1152], P('tensor'), may hold values from -0.078125 to 0.078125
- g_ffn_post: float32 [1152], replicated, may hold values from 0.5 to 1.5
- cotangent: bfloat16 [2, 8192, 1152], P(None, 'dp'), may hold values from -6 to 6
Outputs:
- output: bfloat16 [2, 8192, 1152], P(None, 'dp')
- grad_input: float32 [2, 8192, 1152], P(None, 'dp')
- grad_g_attn_in: float32 [1152], P('dp')
- grad_w_query: float32 [1152, 1024], P('dp', 'tensor')
- grad_w_key: float32 [1152, 256], P('dp')
- grad_w_value: float32 [1152, 256], P('dp')
- grad_g_query: float32 [256], P('dp')
- grad_g_key: float32 [256], P('dp')
- grad_w_out: float32 [1024, 1152], P('tensor', 'dp')
- grad_g_attn_post: float32 [1152], P('dp')
- grad_g_ffn_in: float32 [1152], P('dp')
- grad_w_gate: float32 [1152, 6912], P('dp', 'tensor')
- grad_w_up: float32 [1152, 6912], P('dp', 'tensor')
- grad_w_down: float32 [6912, 1152], P('tensor', 'dp')
- grad_g_ffn_post: float32 [1152], P('dp')
Inputs may be any that keep to these rules, and one draw needn't show every extreme that they name: `image_starts`: each aligned block of 512 tokens holds exactly one image span of 256 tokens, starting this many tokens into the block.
All inputs are finite; a program needn't handle non-finite values.
Results may differ from a plain program's by a relative error of at most 0.019.
Values may be sent and summed in bfloat16 or wider, within the bound.
No kernel may reach another device: no remote copies, remote signals or barrier semaphores. Data moves between devices by JAX's collectives and lax.ppermute only.
A program may use at most 384 MiB of HBM per device.

v0:
```python
from functools import partial

import jax
import jax.numpy as jnp
from jax import lax
from jax.sharding import PartitionSpec as P

HD = 256
WINDOW = 512
IMG = 256
SEQ_LEN = 4096


EPSILON = 1e-06
NEGATIVE = -1e30


def from_behind(value, axis, steps):
    count = lax.axis_size(axis)
    initial, last = (max(0, -steps), min(count, count - steps))
    return lax.ppermute(value, axis, [(source, source + steps) for source in range(initial, last)])


def norm_rows(values, gain):
    return values * lax.rsqrt(jnp.mean(values * values, axis=-1, keepdims=True) + EPSILON) * gain


def rotate(values, cosine, sine_table):
    half_width = values.shape[-1] // 2
    front_half = values[..., :half_width]
    back_half = values[..., half_width:]
    return jnp.concatenate(
        [
            front_half * cosine - back_half * sine_table,
            back_half * cosine + front_half * sine_table,
        ],
        axis=-1,
    )


def angle_tables(places):
    half_width = HD // 2
    frequency = 10000.0 ** (-2.0 * jnp.arange(half_width, dtype=jnp.float32) / HD)
    angles = places.astype(jnp.float32)[:, None] * frequency[None, :]
    return (jnp.cos(angles), jnp.sin(angles))


def in_span(offsets, row_count):
    relative = jnp.arange(row_count, dtype=jnp.int32) % WINDOW
    starts = jnp.repeat(offsets, WINDOW)
    return (relative >= starts) & (relative < starts + IMG)


def block_mask(query_local, key_local, span_query, span_key, seq_offset):
    causal = (key_local[None, :] <= query_local[:, None]) & (
        query_local[:, None] - key_local[None, :] < WINDOW
    )
    same_block = key_local[None, :] // WINDOW == query_local[:, None] // WINDOW
    image = span_query[:, None] & span_key[None, :] & same_block
    return (key_local[None, :] + seq_offset >= 0) & (causal | image)


def query_piece(query_raw, gain, cosine, sine_table):
    return rotate(norm_rows(query_raw, gain), cosine[:, None, :], sine_table[:, None, :]) * HD ** (
        -0.5
    )


def key_piece(key_raw, gain, cosine, sine_table):
    return rotate(norm_rows(key_raw, gain), cosine, sine_table)


def gated_gelu(gate_all, up_all):
    return jax.nn.gelu(gate_all, approximate=True) * up_all


def add_rows(running, addition):
    return running + addition


def shards(
    tokens,
    image_starts,
    g_attn_in,
    w_query,
    w_key,
    w_value,
    g_query,
    g_key,
    w_out,
    g_attn_post,
    g_ffn_in,
    w_gate,
    w_up,
    w_down,
    g_ffn_post,
    cotangent,
):
    row_count = tokens.shape[1]
    head_count = w_query.shape[1] // HD
    block_count = row_count // WINDOW
    seq_offset = lax.axis_index("dp") % (SEQ_LEN // row_count) * row_count
    cosine, sine_table = angle_tables(seq_offset + jnp.arange(row_count, dtype=jnp.int32))
    first_tensor = (lax.axis_index("tensor") == 0).astype(jnp.float32)
    local_rows = jnp.arange(WINDOW, dtype=jnp.int32)
    window_rows = jnp.arange(2 * WINDOW, dtype=jnp.int32)
    query_rule = partial(query_piece, cosine=cosine, sine_table=sine_table)
    key_rule = partial(key_piece, cosine=cosine, sine_table=sine_table)
    learned = (
        g_attn_in,
        w_query,
        w_key,
        w_value,
        g_query,
        g_key,
        w_out,
        g_attn_post,
        g_ffn_in,
        w_gate,
        w_up,
        w_down,
        g_ffn_post,
    )
    start_totals = tuple((jnp.zeros(element.shape, jnp.float32) for element in learned))

    def micro_step(totals, inputs):
        token_rows, start_row, cotangent_rows = inputs
        source = token_rows.astype(jnp.float32)
        in_image = in_span(start_row, row_count)
        image_ext = jnp.concatenate([jnp.zeros((WINDOW,), jnp.bool_), in_image], 0)
        normed_f32, pull_attn_in = jax.vjp(norm_rows, source, g_attn_in)
        normed = normed_f32.astype(jnp.bfloat16)
        query_raw = jnp.dot(normed, w_query, preferred_element_type=jnp.float32).reshape(
            row_count, head_count, HD
        )
        key_raw = jnp.dot(normed, w_key, preferred_element_type=jnp.float32)
        value_low = jnp.dot(normed, w_value, preferred_element_type=jnp.float32).astype(
            jnp.bfloat16
        )
        query_f32, pull_query = jax.vjp(query_rule, query_raw, g_query)
        key_f32, pull_key = jax.vjp(key_rule, key_raw, g_key)
        query_low = query_f32.astype(jnp.bfloat16)
        key_low = key_f32.astype(jnp.bfloat16)
        key_near, value_near = from_behind((key_low, value_low), "dp", 1)
        key_ext = jnp.concatenate([key_near, key_low], 0)
        value_ext = jnp.concatenate([value_near, value_low], 0)

        def window_parts(block_index):
            first_row = block_index * WINDOW
            valid = block_mask(
                first_row + local_rows,
                first_row - WINDOW + window_rows,
                in_image,
                image_ext,
                seq_offset,
            )
            scores = jnp.einsum(
                "qhd,kd->hqk", query_low, key_ext, preferred_element_type=jnp.float32
            )
            return (
                first_row,
                query_low,
                key_ext,
                value_ext,
                jnp.where(valid[None], scores, NEGATIVE),
            )

        def forward_block(block_index):
            first_row, query_block, key_window, value_window, scores = window_parts(block_index)
            row_peak = jnp.max(scores, axis=-1, keepdims=True)
            log_total = row_peak + jnp.log(
                jnp.sum(jnp.exp(scores - row_peak), axis=-1, keepdims=True)
            )
            probs_low = jnp.exp(scores - log_total).astype(jnp.bfloat16)
            return (
                jnp.einsum(
                    "hqk,kd->qhd", probs_low, value_window, preferred_element_type=jnp.float32
                ),
                log_total,
            )

        mixed_blocks, log_totals = lax.map(forward_block, jnp.arange(block_count, dtype=jnp.int32))
        mixed_low = mixed_blocks.reshape(row_count, head_count * HD).astype(jnp.bfloat16)
        branch = lax.psum(jnp.dot(mixed_low, w_out, preferred_element_type=jnp.float32), "tensor")
        post_attn, pull_attn_post = jax.vjp(norm_rows, branch, g_attn_post)
        middle = source + post_attn
        normed_ffn_f32, pull_ffn_in = jax.vjp(norm_rows, middle, g_ffn_in)
        normed_ffn = normed_ffn_f32.astype(jnp.bfloat16)
        gate_all = jnp.dot(normed_ffn, w_gate, preferred_element_type=jnp.float32)
        up_all = jnp.dot(normed_ffn, w_up, preferred_element_type=jnp.float32)
        hidden_f32, pull_hidden = jax.vjp(gated_gelu, gate_all, up_all)
        hidden_low = hidden_f32.astype(jnp.bfloat16)
        ffn_out = lax.psum(
            jnp.dot(hidden_low, w_down, preferred_element_type=jnp.float32), "tensor"
        )
        post_ffn, pull_ffn_post = jax.vjp(norm_rows, ffn_out, g_ffn_post)
        final_f32 = middle + post_ffn
        upstream = cotangent_rows.astype(jnp.float32)
        ffn_grad, grad_ffn_post = pull_ffn_post(upstream)
        ffn_grad_low = ffn_grad.astype(jnp.bfloat16)
        grad_down = jnp.einsum(
            "tf,td->fd", hidden_low, ffn_grad_low, preferred_element_type=jnp.float32
        )
        hidden_grad = jnp.einsum(
            "td,fd->tf", ffn_grad_low, w_down, preferred_element_type=jnp.float32
        )
        gate_grad, up_grad = pull_hidden(hidden_grad)
        gate_grad_low = gate_grad.astype(jnp.bfloat16)
        up_grad_low = up_grad.astype(jnp.bfloat16)
        grad_gate = jnp.einsum(
            "td,tf->df", normed_ffn, gate_grad_low, preferred_element_type=jnp.float32
        )
        grad_up = jnp.einsum(
            "td,tf->df", normed_ffn, up_grad_low, preferred_element_type=jnp.float32
        )
        normed_ffn_grad = jnp.einsum(
            "tf,df->td", gate_grad_low, w_gate, preferred_element_type=jnp.float32
        ) + jnp.einsum("tf,df->td", up_grad_low, w_up, preferred_element_type=jnp.float32)
        middle_part, ffn_gain_part = pull_ffn_in(normed_ffn_grad)
        middle_sum, grad_ffn_in = lax.psum((middle_part, ffn_gain_part), "tensor")
        middle_grad = upstream + middle_sum
        branch_grad, grad_attn_post = pull_attn_post(middle_grad)
        branch_grad_low = branch_grad.astype(jnp.bfloat16)
        grad_out = jnp.einsum(
            "te,td->ed", mixed_low, branch_grad_low, preferred_element_type=jnp.float32
        )
        mixed_grad_low = (
            jnp.einsum("td,ed->te", branch_grad_low, w_out, preferred_element_type=jnp.float32)
            .astype(jnp.bfloat16)
            .reshape(row_count, head_count, HD)
        )

        def backward_block(carry, block_index):
            key_grad, value_grad = carry
            first_row, query_block, key_window, value_window, scores = window_parts(block_index)
            probs_f32 = jnp.exp(scores - log_totals[block_index])
            probs_low = probs_f32.astype(jnp.bfloat16)
            probs_grad = jnp.einsum(
                "qhd,kd->hqk", mixed_grad_low, value_window, preferred_element_type=jnp.float32
            )
            row_dot = jnp.sum(probs_f32 * probs_grad, axis=-1, keepdims=True)
            scores_grad = (probs_f32 * (probs_grad - row_dot)).astype(jnp.bfloat16)
            query_grad = jnp.einsum(
                "hqk,kd->qhd", scores_grad, key_window, preferred_element_type=jnp.float32
            )
            key_grad = add_rows(
                key_grad,
                jnp.einsum(
                    "hqk,qhd->kd", scores_grad, query_block, preferred_element_type=jnp.float32
                ),
            )
            value_grad = add_rows(
                value_grad,
                jnp.einsum(
                    "hqk,qhd->kd", probs_low, mixed_grad_low, preferred_element_type=jnp.float32
                ),
            )
            return ((key_grad, value_grad), query_grad)

        empty_ext = jnp.zeros((row_count + WINDOW, HD), jnp.float32)
        (key_grad_ext, value_grad_ext), query_grads = lax.scan(
            backward_block, (empty_ext, empty_ext), jnp.arange(block_count, dtype=jnp.int32)
        )
        back_key, back_value = (
            from_behind(key_grad_ext[:WINDOW].astype(jnp.bfloat16), "dp", -1).astype(jnp.float32),
            from_behind(value_grad_ext[:WINDOW].astype(jnp.bfloat16), "dp", -1).astype(jnp.float32),
        )
        key_own = key_grad_ext[WINDOW:].at[row_count - WINDOW :].add(back_key)
        value_own = value_grad_ext[WINDOW:].at[row_count - WINDOW :].add(back_value)
        key_total, value_total = (
            lax.psum(key_own.astype(jnp.bfloat16), "tensor").astype(jnp.float32),
            lax.psum(value_own.astype(jnp.bfloat16), "tensor").astype(jnp.float32),
        )
        value_grad_low = value_total.astype(jnp.bfloat16)
        key_raw_grad, grad_key_gain = pull_key(key_total)
        key_grad_low = key_raw_grad.astype(jnp.bfloat16)
        query_raw_grad, query_gain_part = pull_query(query_grads.reshape(row_count, head_count, HD))
        query_grad_low = query_raw_grad.astype(jnp.bfloat16).reshape(row_count, head_count * HD)
        grad_query = jnp.einsum(
            "td,te->de", normed, query_grad_low, preferred_element_type=jnp.float32
        )
        grad_key = jnp.einsum("td,tk->dk", normed, key_grad_low, preferred_element_type=jnp.float32)
        grad_value = jnp.einsum(
            "td,tk->dk", normed, value_grad_low, preferred_element_type=jnp.float32
        )
        shared_grad = jnp.einsum(
            "tk,dk->td", key_grad_low, w_key, preferred_element_type=jnp.float32
        ) + jnp.einsum("tk,dk->td", value_grad_low, w_value, preferred_element_type=jnp.float32)
        normed_grad = (
            jnp.einsum("te,de->td", query_grad_low, w_query, preferred_element_type=jnp.float32)
            + first_tensor * shared_grad
        )
        source_part, attn_gain_part = pull_attn_in(normed_grad)
        source_sum, grad_attn_in, grad_query_gain = (
            lax.psum(source_part.astype(jnp.bfloat16), "tensor").astype(jnp.float32),
            lax.psum(attn_gain_part.astype(jnp.bfloat16), "tensor").astype(jnp.float32),
            lax.psum(query_gain_part.astype(jnp.bfloat16), "tensor").astype(jnp.float32),
        )
        input_grad = middle_grad + source_sum
        step_grads = (
            grad_attn_in,
            grad_query,
            grad_key,
            grad_value,
            grad_query_gain,
            grad_key_gain,
            grad_out,
            grad_attn_post,
            grad_ffn_in,
            grad_gate,
            grad_up,
            grad_down,
            grad_ffn_post,
        )
        totals = tuple((running + portion for running, portion in zip(totals, step_grads)))
        return (totals, (final_f32.astype(jnp.bfloat16), input_grad))

    totals, (outputs, input_grads) = lax.scan(
        micro_step, start_totals, (tokens, image_starts, cotangent)
    )
    shares = (
        lax.psum_scatter(totals[0], "dp", scatter_dimension=0, tiled=True),
        lax.psum_scatter(totals[1], "dp", scatter_dimension=0, tiled=True),
        lax.psum_scatter(totals[2], "dp", scatter_dimension=0, tiled=True),
        lax.psum_scatter(totals[3], "dp", scatter_dimension=0, tiled=True),
        lax.psum_scatter(totals[4], "dp", scatter_dimension=0, tiled=True),
        lax.psum_scatter(totals[5], "dp", scatter_dimension=0, tiled=True),
        lax.psum_scatter(totals[6], "dp", scatter_dimension=1, tiled=True),
        lax.psum_scatter(totals[7], "dp", scatter_dimension=0, tiled=True),
        lax.psum_scatter(totals[8], "dp", scatter_dimension=0, tiled=True),
        lax.psum_scatter(totals[9], "dp", scatter_dimension=0, tiled=True),
        lax.psum_scatter(totals[10], "dp", scatter_dimension=0, tiled=True),
        lax.psum_scatter(totals[11], "dp", scatter_dimension=1, tiled=True),
        lax.psum_scatter(totals[12], "dp", scatter_dimension=0, tiled=True),
    )
    return (
        outputs,
        input_grads,
        shares[0],
        shares[1],
        shares[2],
        shares[3],
        shares[4],
        shares[5],
        shares[6],
        shares[7],
        shares[8],
        shares[9],
        shares[10],
        shares[11],
        shares[12],
    )


def solution(mesh):
    in_specs = (
        P(None, "dp", None),
        P(None, "dp"),
        P(),
        P(None, "tensor"),
        P(),
        P(),
        P(),
        P(),
        P("tensor", None),
        P(),
        P(),
        P(None, "tensor"),
        P(None, "tensor"),
        P("tensor", None),
        P(),
        P(None, "dp", None),
    )
    out_specs = (
        P(None, "dp", None),
        P(None, "dp", None),
        P("dp"),
        P("dp", "tensor"),
        P("dp", None),
        P("dp", None),
        P("dp"),
        P("dp"),
        P("tensor", "dp"),
        P("dp"),
        P("dp"),
        P("dp", "tensor"),
        P("dp", "tensor"),
        P("tensor", "dp"),
        P("dp"),
    )
    return jax.shard_map(shards, mesh=mesh, in_specs=in_specs, out_specs=out_specs, check_vma=False)
```

profile of v0, /device:TPU:0, one launch (start us, length us, event | category | flops | bytes accessed | tf_op | source)
XLA Modules:
  0.0 1656.1 jit_solution(6189537121492937075)
XLA Ops:
  11.0 854.8 %while.61 = (s32[]{:T(128)}, f32[1152]{0:T(1024)}, f32[1152,512]{1,0:T(8,128)}, f32[1152,256]{1,0:T(8,128)}, f32[1152,256]{1,0:T(8,128)}, /*index=5*/f32[256]{0:...) while((s32[]{:T(128)}, f32[1152]{0:T(1024)}, ...), condition=%wide.region_31.32_spmd.clone.clone.clone.clone, body=%wide.region_0.31_spmd.clone.clone.clone.clone.sunk | while | flops 45551083520 | bytes 789225536 | solution.py:318
  45.2 68.2 %all-reduce.27.cloned.1.call-done = f32[512,1152]{1,0:T(8,128)} async-done(((f32[512,1152]{1,0:T(8,128)}), f32[512,1152]{1,0:T(8,128)}) %all-reduce.27.cloned.1.call-update) | async-done | bytes 2359312 | tf_op jit(solution)/shard_map/while/body/eval_jaxpr/psum | solution.py:184
  118.5 10.3 fusion.304
  128.8 9.1 multiply_convert_fusion.7
  146.2 68.5 %all-reduce.29.cloned.1.call-done = f32[512,1152]{1,0:T(8,128)} async-done(((f32[512,1152]{1,0:T(8,128)}), f32[512,1152]{1,0:T(8,128)}) %all-reduce.29.cloned.1.call-update) | async-done | bytes 2359312 | tf_op jit(solution)/shard_map/while/body/eval_jaxpr/psum | solution.py:193
  220.5 16.2 multiply_convert_fusion.8
  236.7 9.4 fusion.308
  246.2 9.1 multiply_reduce_fusion.27
  257.7 10.3 convolution_add_fusion.20
  294.4 31.8 %all-reduce.31.cloned.1.call-done = f32[512,1152]{1,0:T(8,128)} async-done(((f32[512,1152]{1,0:T(8,128)}), f32[512,1152]{1,0:T(8,128)}) %all-reduce.31.cloned.1.call-update) | async-done | bytes 2359312 | tf_op jit(solution)/shard_map/while/body/eval_jaxpr/psum | solution.py:220
  357.1 27.1 %all-reduce.33.cloned.1.call-done = (bf16[512,256]{0,1:T(8,128)(2,1)}, bf16[512,256]{1,0:T(8,128)(2,1)}) async-done(((bf16[512,256]{0,1:T(8,128)(2,1)}, bf16[512,256]{1,0:T(8,128)(2,1)}), (bf16[512,256]{0,1:T(8,128)(2,1)}, bf16[512,256]{1,0:T(8,128)(2,1)})) %all-reduce.33.cloned.1.call-update) | async-done | bytes 524304 | tf_op jit(solution)/shard_map/while/body/eval_jaxpr/psum | solution.py:271
  399.9 34.6 %all-reduce.35.cloned.1.call-done = bf16[512,1152]{1,0:T(8,128)(2,1)} async-done(((bf16[512,1152]{1,0:T(8,128)(2,1)}), bf16[512,1152]{1,0:T(8,128)(2,1)}) %all-reduce.35.cloned.1.call-update) | async-done | bytes 1179664 | tf_op jit(solution)/shard_map/while/body/eval_jaxpr/psum | solution.py:295
  471.4 66.7 %all-reduce.27.cloned.1.call-done = f32[512,1152]{1,0:T(8,128)} async-done(((f32[512,1152]{1,0:T(8,128)}), f32[512,1152]{1,0:T(8,128)}) %all-reduce.27.cloned.1.call-update) | async-done | bytes 2359312 | tf_op jit(solution)/shard_map/while/body/eval_jaxpr/psum | solution.py:184
  543.1 10.3 fusion.304
  570.8 68.6 %all-reduce.29.cloned.1.call-done = f32[512,1152]{1,0:T(8,128)} async-done(((f32[512,1152]{1,0:T(8,128)}), f32[512,1152]{1,0:T(8,128)}) %all-reduce.29.cloned.1.call-update) | async-done | bytes 2359312 | tf_op jit(solution)/shard_map/while/body/eval_jaxpr/psum | solution.py:193
  645.2 16.2 multiply_convert_fusion.8
  661.4 9.4 fusion.308
  670.8 9.1 multiply_reduce_fusion.27
  682.2 15.9 convolution_add_fusion.20
  698.0 11.2 convolution_add_fusion.21
  720.4 12.6 convolution_add_fusion.22
  733.0 17.8 %all-reduce.31.cloned.1.call-done = f32[512,1152]{1,0:T(8,128)} async-done(((f32[512,1152]{1,0:T(8,128)}), f32[512,1152]{1,0:T(8,128)}) %all-reduce.31.cloned.1.call-update) | async-done | bytes 2359312 | tf_op jit(solution)/shard_map/while/body/eval_jaxpr/psum | solution.py:220
  782.7 26.4 %all-reduce.33.cloned.1.call-done = (bf16[512,256]{0,1:T(8,128)(2,1)}, bf16[512,256]{1,0:T(8,128)(2,1)}) async-done(((bf16[512,256]{0,1:T(8,128)(2,1)}, bf16[512,256]{1,0:T(8,128)(2,1)}), (bf16[512,256]{0,1:T(8,128)(2,1)}, bf16[512,256]{1,0:T(8,128)(2,1)})) %all-reduce.33.cloned.1.call-update) | async-done | bytes 524304 | tf_op jit(solution)/shard_map/while/body/eval_jaxpr/psum | solution.py:271
  827.5 31.9 %all-reduce.35.cloned.1.call-done = bf16[512,1152]{1,0:T(8,128)(2,1)} async-done(((bf16[512,1152]{1,0:T(8,128)(2,1)}), bf16[512,1152]{1,0:T(8,128)(2,1)}) %all-reduce.35.cloned.1.call-update) | async-done | bytes 1179664 | tf_op jit(solution)/shard_map/while/body/eval_jaxpr/psum | solution.py:295
  870.3 17.2 %copy.56 = f32[3456,1152]{0,1:T(8,128)} copy(f32[3456,1152]{1,0:T(8,128)} %get-tuple-element.2012) | data formatting | bytes 31850496 | tf_op jit(solution)/shard_map/while | solution.py:318
  890.9 61.3 %all-reduce.16 = (f32[1152]{0:T(1024)S(1)}, f32[256]{0:T(256)S(1)}, f32[256]{0:T(256)S(1)}, f32[1152]{0:T(1024)S(1)}, f32[1152]{0:T(1024)S(1)}, /*index=5*/f32[1152]{0:T(1024)S(1)}) all-reduce(f32[1152]{0:T(1024)S(1)} %copy-done.88, f32[256]{0:T(256)S(1)} %copy-done.102, ...), channel_id=2, replica_groups=mesh['dp'=16,'tensor'=2] {'dp'}, use_global_device_ids=true, to_apply=%region_32.33.clone | all-reduce | flops 5120 | bytes 40960
  955.8 34.0 %reduce-scatter.18.cloned.1.call-done = f32[72,256]{1,0:T(8,128)} async-done(((f32[1152,256]{1,0:T(8,128)}), f32[72,256]{1,0:T(8,128)}) %reduce-scatter.18.cloned.1.call-update) | async-done | bytes 73744 | tf_op jit(solution)/shard_map/reduce_scatter | solution.py:325
  989.8 66.1 %reduce-scatter.20.cloned.1.call-done = f32[512,72]{0,1:T(8,128)} async-done(((f32[512,1152]{0,1:T(8,128)}), f32[512,72]{0,1:T(8,128)}) %reduce-scatter.20.cloned.1.call-update) | async-done | bytes 147472 | tf_op jit(solution)/shard_map/reduce_scatter | solution.py:328
  1055.8 66.7 %reduce-scatter.14.cloned.1.call-done = f32[72,512]{1,0:T(8,128)} async-done(((f32[1152,512]{1,0:T(8,128)}), f32[72,512]{1,0:T(8,128)}) %reduce-scatter.14.cloned.1.call-update) | async-done | bytes 147472 | tf_op jit(solution)/shard_map/reduce_scatter | solution.py:323
  1122.6 175.3 %reduce-scatter.26.cloned.1.call-done = f32[3456,72]{0,1:T(8,128)} async-done(((f32[3456,1152]{0,1:T(8,128)}), f32[3456,72]{0,1:T(8,128)}) %reduce-scatter.26.cloned.1.call-update) | async-done | bytes 995344
  1297.8 175.4 %reduce-scatter.22.cloned.1.call-done = f32[72,3456]{1,0:T(8,128)} async-done(((f32[1152,3456]{1,0:T(8,128)}), f32[72,3456]{1,0:T(8,128)}) %reduce-scatter.22.cloned.1.call-update) | async-done | bytes 995344
  1473.2 175.2 %reduce-scatter.24.cloned.1.call-done = f32[72,3456]{1,0:T(8,128)} async-done(((f32[1152,3456]{1,0:T(8,128)}), f32[72,3456]{1,0:T(8,128)}) %reduce-scatter.24.cloned.1.call-update) | async-done | bytes 995344
  (664 shorter events, 269.8 us)
Async XLA Ops:
  11.5 101.9 %all-reduce.27.cloned.1.call-start = ((), (), s32[]{:S(2)}) async-start(), calls=%async_computation.14 | async-start | bytes 4718592 | tf_op jit(solution)/shard_map/while/body/eval_jaxpr/psum | solution.py:184
  17.2 18.3 %collective-permute-start = (bf16[512,256]{0,1:T(8,128)(2,1)}, bf16[512,256]{0,1:T(8,128)(2,1)}, u32[]{:S(2)}, u32[]{:S(2)}) collective-permute-start(bf16[512,256]{0,1:T(8,128)(2,1)} %pad_maximum_fusion.2), channel_id=1, source_target_pairs={{0,2},{2,4},{4,6},{6,8},{8,10},{10,12},{12,14},{14,16},{16,18},{18... | collective-permute-start | bytes 786440 | tf_op jit(solution)/shard_map/while/body/eval_jaxpr/ppermute | solution.py:21
  21.5 17.0 %collective-permute-start.1 = (bf16[512,256]{1,0:T(8,128)(2,1)}, bf16[512,256]{1,0:T(8,128)(2,1)}, u32[]{:S(2)}, u32[]{:S(2)}) collective-permute-start(bf16[512,256]{1,0:T(8,128)(2,1)} %convolution_convert_fusion.6), channel_id=1, source_target_pairs={{0,2},{2,4},{4,6},{6,8},{8,10},{10,12},{12,14},{14,16},{16,18},{18... | collective-permute-start | bytes 786440 | tf_op jit(solution)/shard_map/while/body/eval_jaxpr/ppermute | solution.py:21
  45.0 71.0 %copy-start.53 = (f32[1152]{0:T(1024)S(1)}, f32[1152]{0:T(1024)}, u32[]{:S(2)}) copy-start(f32[1152]{0:T(1024)} %get-tuple-element.1898) | copy-start | bytes 13828 | tf_op jit(solution)/shard_map/while
  45.0 169.7 %all-reduce.29.cloned.1.call-start = ((), (), s32[]{:S(2)}) async-start(), calls=%async_computation.15 | async-start | bytes 4718592 | tf_op jit(solution)/shard_map/while/body/eval_jaxpr/psum | solution.py:193
  145.9 180.3 %all-reduce.31.cloned.1.call-start = ((), (), s32[]{:S(2)}) async-start(), calls=%async_computation.16 | async-start | bytes 4718592 | tf_op jit(solution)/shard_map/while/body/eval_jaxpr/psum | solution.py:220
  257.2 126.9 %all-reduce.33.cloned.1.call-start = ((), (), s32[]{:S(2)}) async-start(), calls=%async_computation.17 | async-start | bytes 1048576 | tf_op jit(solution)/shard_map/while/body/eval_jaxpr/psum | solution.py:271
  285.7 40.5 %copy-start.70 = (f32[512]{0:T(512)S(1)}, f32[512]{0:T(512)}, u32[]{:S(2)}) copy-start(f32[512]{0:T(512)} %copy-done.69) | copy-start | bytes 6148 | tf_op jit(solution)/shard_map/while
  294.4 36.0 %copy-start.76 = (f32[512]{0:T(512)S(1)}, f32[512]{0:T(512)}, u32[]{:S(2)}) copy-start(f32[512]{0:T(512)} %copy-done.75) | copy-start | bytes 6148 | tf_op jit(solution)/shard_map/while
  294.4 36.0 %copy-start.4 = (f32[512,1152]{1,0:T(8,128)S(1)}, f32[512,1152]{1,0:T(8,128)}, u32[]{:S(2)}) copy-start(f32[512,1152]{1,0:T(8,128)} %all-reduce.27.cloned.1.call-done) | copy-start | bytes 7077892 | tf_op jit(solution)/shard_map/while
  335.1 16.6 %collective-permute-start.3 = (bf16[512,256]{1,0:T(8,128)(2,1)S(1)}, bf16[512,256]{1,0:T(8,128)(2,1)S(1)}, u32[]{:S(2)}, u32[]{:S(2)}) collective-permute-start(bf16[512,256]{1,0:T(8,128)(2,1)S(1)} %slice.163), channel_id=1, source_target_pairs={{2,0},{4,2},{6,4},{8,6},{10,8},{12,10},{14,12},{16,14},{18,16},{20... | collective-permute-start | bytes 786440 | tf_op jit(solution)/shard_map/while/body/eval_jaxpr/ppermute | solution.py:21
  341.2 11.4 collective-permute-start.2
  353.3 81.2 %all-reduce.35.cloned.1.call-start = ((), (), s32[]{:S(2)}) async-start(), calls=%async_computation.18 | async-start | bytes 2359296 | tf_op jit(solution)/shard_map/while/body/eval_jaxpr/psum | solution.py:295
  438.9 99.3 %all-reduce.27.cloned.1.call-start = ((), (), s32[]{:S(2)}) async-start(), calls=%async_computation.14 | async-start | bytes 4718592 | tf_op jit(solution)/shard_map/while/body/eval_jaxpr/psum | solution.py:184
  444.5 16.8 %collective-permute-start = (bf16[512,256]{0,1:T(8,128)(2,1)}, bf16[512,256]{0,1:T(8,128)(2,1)}, u32[]{:S(2)}, u32[]{:S(2)}) collective-permute-start(bf16[512,256]{0,1:T(8,128)(2,1)} %pad_maximum_fusion.2), channel_id=1, source_target_pairs={{0,2},{2,4},{4,6},{6,8},{8,10},{10,12},{12,14},{14,16},{16,18},{18... | collective-permute-start | bytes 786440 | tf_op jit(solution)/shard_map/while/body/eval_jaxpr/ppermute | solution.py:21
  448.2 16.1 collective-permute-start.1
  470.9 69.8 %copy-start.53 = (f32[1152]{0:T(1024)S(1)}, f32[1152]{0:T(1024)}, u32[]{:S(2)}) copy-start(f32[1152]{0:T(1024)} %get-tuple-element.1898) | copy-start | bytes 13828 | tf_op jit(solution)/shard_map/while
  470.9 168.5 %all-reduce.29.cloned.1.call-start = ((), (), s32[]{:S(2)}) async-start(), calls=%async_computation.15 | async-start | bytes 4718592 | tf_op jit(solution)/shard_map/while/body/eval_jaxpr/psum | solution.py:193
  570.6 180.3 %all-reduce.31.cloned.1.call-start = ((), (), s32[]{:S(2)}) async-start(), calls=%async_computation.16 | async-start | bytes 4718592 | tf_op jit(solution)/shard_map/while/body/eval_jaxpr/psum | solution.py:220
  681.9 127.2 %all-reduce.33.cloned.1.call-start = ((), (), s32[]{:S(2)}) async-start(), calls=%async_computation.17 | async-start | bytes 1048576 | tf_op jit(solution)/shard_map/while/body/eval_jaxpr/psum | solution.py:271
  759.8 16.9 %collective-permute-start.3 = (bf16[512,256]{1,0:T(8,128)(2,1)S(1)}, bf16[512,256]{1,0:T(8,128)(2,1)S(1)}, u32[]{:S(2)}, u32[]{:S(2)}) collective-permute-start(bf16[512,256]{1,0:T(8,128)(2,1)S(1)} %slice.163), channel_id=1, source_target_pairs={{2,0},{4,2},{6,4},{8,6},{10,8},{12,10},{14,12},{16,14},{18,16},{20... | collective-permute-start | bytes 786440 | tf_op jit(solution)/shard_map/while/body/eval_jaxpr/ppermute | solution.py:21
  766.1 11.3 collective-permute-start.2
  778.2 81.2 %all-reduce.35.cloned.1.call-start = ((), (), s32[]{:S(2)}) async-start(), calls=%async_computation.18 | async-start | bytes 2359296 | tf_op jit(solution)/shard_map/while/body/eval_jaxpr/psum | solution.py:295
  778.3 33.0 %copy-start.19 = (f32[512,256]{0,1:T(8,128)S(1)}, f32[512,256]{0,1:T(8,128)}, u32[]{:S(2)}) copy-start(f32[512,256]{0,1:T(8,128)} %copy-done.18) | copy-start | bytes 1572868 | tf_op jit(solution)/shard_map/while
  778.4 33.0 %copy-start.62 = (f32[512]{0:T(512)S(1)}, f32[512]{0:T(512)}, u32[]{:S(2)}) copy-start(f32[512]{0:T(512)} %copy-done.61) | copy-start | bytes 6148 | tf_op jit(solution)/shard_map/while
  865.9 89.9 %reduce-scatter.16.cloned.1.call-start = ((), (), s32[]{:S(2)}) async-start(), calls=%async_computation.8 | async-start | bytes 1253376 | tf_op jit(solution)/shard_map/reduce_scatter | solution.py:324
  866.5 123.3 %reduce-scatter.18.cloned.1.call-start = ((), (), s32[]{:S(2)}) async-start(), calls=%async_computation.9 | async-start | bytes 1253376 | tf_op jit(solution)/shard_map/reduce_scatter | solution.py:325
  867.1 188.8 %reduce-scatter.20.cloned.1.call-start = ((), (), s32[]{:S(2)}) async-start(), calls=%async_computation.10 | async-start | bytes 2506752 | tf_op jit(solution)/shard_map/reduce_scatter | solution.py:328
  869.6 253.0 %reduce-scatter.14.cloned.1.call-start = ((), (), s32[]{:S(2)}) async-start(), calls=%async_computation.7 | async-start | bytes 2506752 | tf_op jit(solution)/shard_map/reduce_scatter | solution.py:323
  870.3 427.5 %reduce-scatter.26.cloned.1.call-start = ((), (), s32[]{:S(2)}) async-start(), calls=%async_computation.13 | async-start | bytes 16920576
  887.6 585.7 %reduce-scatter.22.cloned.1.call-start = ((), (), s32[]{:S(2)}) async-start(), calls=%async_computation.11 | async-start | bytes 16920576
  888.3 760.1 %reduce-scatter.24.cloned.1.call-start = ((), (), s32[]{:S(2)}) async-start(), calls=%async_computation.12 | async-start | bytes 16920576
  (206 other events, 1171.1 us)
Sparse Core Ops, SparseCore 0:
  45.1 68.2 all-reduce.26
  146.0 68.6 all-reduce.28
  257.3 68.8 all-reduce.30
  353.4 30.6 all-reduce.32
  391.6 42.8 all-reduce.34
  471.0 67.0 all-reduce.26
  570.7 68.6 all-reduce.28
  682.0 68.8 all-reduce.30
  778.3 30.6 all-reduce.32
  816.5 42.9 all-reduce.34
Sparse Core Ops, SparseCore 1:
  870.5 58.0 reduce-scatter.15
  932.7 57.0 reduce-scatter.17
  994.0 61.8 reduce-scatter.19
  1060.7 61.8 reduce-scatter.13
  1127.3 170.5 reduce-scatter.25
  1302.5 170.6 reduce-scatter.21
  1477.8 170.6 reduce-scatter.23
where the time goes:
time: 1660 us
  waiting for transfers between devices  1140 us (69%)
  matrix products  253 us (15%)
  other arithmetic  87 us (5%)
  blocking collectives  81.8 us (5%)
  local copies, waits for them, and re-layouts  50.4 us (3%)
  starting transfers between devices  22 us (1%)
  between operations  17.4 us (1%)
    unnamed x10, waiting for transfers between devices  529 us
    psum x2, waiting for transfers between devices, micro_step(): lax.psum(jnp.dot(hidden_low, w_down, preferred_element_type=jnp.float32),...  137 us
    psum x2, waiting for transfers between devices, micro_step(): lax.psum(jnp.dot(mixed_low, w_out, preferred_element_type=jnp.float32), '...  135 us
    reduce_scatter x1, waiting for transfers between devices, shards(): lax.psum_scatter(totals[1], 'dp', scatter_dimension=0, tiled=True)  66.7 us
    psum x2, waiting for transfers between devices, micro_step(): lax.psum(source_part.astype(jnp.bfloat16), 'tensor').astype(jnp.float32)  66.5 us
    reduce_scatter x1, waiting for transfers between devices, shards(): lax.psum_scatter(totals[6], 'dp', scatter_dimension=1, tiled=True)  66.1 us
    unnamed x1, blocking collectives  61.3 us
    psum x2, waiting for transfers between devices, micro_step(): lax.psum(key_own.astype(jnp.bfloat16), 'tensor').astype(jnp.float32)  53.4 us
  transfers between devices with their start and end apart: 25, of which 16 were waited for; matrix products, arithmetic and copies ran while one was open for 10% of the time, Pallas kernels for 0%

commit v1 on v0

v1 whole, which is shorter than its diff:
```python
import jax
import jax.numpy as jnp
from jax import lax
from jax.sharding import PartitionSpec as P

HD = 256
WINDOW = 512
IMG = 256
SEQ_LEN = 4096
EPSILON = 1e-06
NEGATIVE = -1e30
F32 = jnp.float32
BF16 = jnp.bfloat16


def dot(a, b, ca=1, cb=0):
    return lax.dot_general(a, b, (((ca,), (cb,)), ((), ())), preferred_element_type=F32)


def inv_rms(v):
    return lax.rsqrt(jnp.mean(v * v, axis=-1, keepdims=True) + EPSILON)


def pull_v(v, r, g, e):
    eg = e * g
    return r * eg - v * (r * r * r) * jnp.mean(v * eg, axis=-1, keepdims=True)


def rotate(v, cosine, sine):
    half = v.shape[-1] // 2
    a, b = v[..., :half], v[..., half:]
    return jnp.concatenate([a * cosine - b * sine, b * cosine + a * sine], axis=-1)


def angle_tables(places):
    half = HD // 2
    frequency = 10000.0 ** (-2.0 * jnp.arange(half, dtype=F32) / HD)
    angles = places.astype(F32)[:, None] * frequency[None, :]
    return jnp.cos(angles), jnp.sin(angles)


def swap_y(v):
    return lax.ppermute(v, "tensor", [(0, 1), (1, 0)])


def swap_dp(v, bit):
    n = lax.axis_size("dp")
    return lax.ppermute(v, "dp", [(i, i ^ (1 << bit)) for i in range(n)])


def shift_dp(v, steps):
    n = lax.axis_size("dp")
    first, last = max(0, -steps), min(n, n - steps)
    return lax.ppermute(v, "dp", [(i, i + steps) for i in range(first, last)])


def bits_of(n):
    return n.bit_length() - 1


def halves_first(a):
    n = lax.axis_size("dp")
    count = bits_of(n)
    t = a.T.reshape((2,) * count + (a.shape[1] // n, a.shape[0]))
    t = t.transpose(tuple(reversed(range(count))) + (count, count + 1))
    return t.reshape(2, a.shape[1] // 2, a.shape[0])


def my_bit(bit):
    return (lax.axis_index("dp") >> bit) & 1


def pick(a, i):
    return lax.dynamic_index_in_dim(a, i, 0, keepdims=False)


def scatter_sum(left, right):
    n = lax.axis_size("dp")
    mine = my_bit(0)
    got = swap_dp(dot(pick(left, 1 - mine), right).astype(BF16), 0)
    total = dot(pick(left, mine), right) + got.astype(F32)
    for bit in range(1, bits_of(n)):
        both = total.astype(BF16).reshape(2, total.shape[0] // 2, total.shape[1])
        mine = my_bit(bit)
        got = swap_dp(pick(both, 1 - mine), bit)
        total = pick(both, mine).astype(F32) + got.astype(F32)
    return total


def shards(
    tokens,
    image_starts,
    g_attn_in,
    w_query,
    w_key,
    w_value,
    g_query,
    g_key,
    w_out,
    g_attn_post,
    g_ffn_in,
    w_gate,
    w_up,
    w_down,
    g_ffn_post,
    cotangent,
):
    mb, rows, width = tokens.shape
    heads_own = w_query.shape[1] // HD
    heads = 2 * heads_own
    y = lax.axis_index("tensor")
    dp = lax.axis_index("dp")
    offset = dp % (SEQ_LEN // rows) * rows
    cosine, sine = angle_tables(offset + jnp.arange(rows, dtype=jnp.int32))
    cos_h, sin_h = cosine[:, None, :], sine[:, None, :]
    scale = HD ** -0.5

    core = my_bit(0)
    halfq = w_query.reshape(2, width // 2, -1)
    halfo = w_out.reshape(2, w_out.shape[0] // 2, width)

    def gather_other(two):
        part = swap_y(pick(two, core))
        other = swap_dp(part, 0)
        pair = jnp.stack([part, other])
        return jnp.concatenate([pick(pair, core), pick(pair, 1 - core)], 0)

    other_q = gather_other(halfq)
    other_o = gather_other(halfo)
    is0 = y == 0
    wq = jnp.where(
        is0,
        jnp.concatenate([w_query, other_q], 1),
        jnp.concatenate([other_q, w_query], 1),
    )
    wo = jnp.where(
        is0,
        jnp.concatenate([w_out, other_o], 0),
        jnp.concatenate([other_o, w_out], 0),
    )

    local = jnp.arange(rows, dtype=jnp.int32)
    window = jnp.arange(2 * rows, dtype=jnp.int32) - rows

    fw = []
    for m in range(mb):
        x = tokens[m].astype(F32)
        r0 = inv_rms(x)
        h1 = (x * r0 * g_attn_in).astype(BF16)
        key_raw = dot(h1, w_key)
        value = dot(h1, w_value).astype(BF16)
        rk = inv_rms(key_raw)
        key = rotate(key_raw * rk * g_key, cosine, sine).astype(BF16)
        near = shift_dp((key, value), 1)
        fw.append((x, r0, h1, key_raw, rk, key, value, near))

    at = []
    for m in range(mb):
        x, r0, h1, key_raw, rk, key, value, near = fw[m]
        query_raw = dot(h1, wq).reshape(rows, heads, HD)
        rq = inv_rms(query_raw)
        query = (rotate(query_raw * rq * g_query, cos_h, sin_h) * scale).astype(BF16)
        keys = jnp.concatenate([near[0], key], 0)
        values = jnp.concatenate([near[1], value], 0)
        start = image_starts[m, 0]
        in_q = (local >= start) & (local < start + IMG)
        in_k = (window >= start) & (window < start + IMG)
        back = local[:, None] - window[None, :]
        valid = ((back >= 0) & (back < WINDOW)) | (in_q[:, None] & in_k[None, :])
        valid = valid & (window[None, :] + offset >= 0)
        scores = jnp.einsum("qhd,kd->hqk", query, keys, preferred_element_type=F32)
        scores = jnp.where(valid[None], scores, NEGATIVE)
        peak = jnp.max(scores, axis=-1, keepdims=True)
        log_total = peak + jnp.log(jnp.sum(jnp.exp(scores - peak), axis=-1, keepdims=True))
        probs = jnp.exp(scores - log_total).astype(BF16)
        mixed = jnp.einsum("hqk,kd->qhd", probs, values, preferred_element_type=F32)
        mixed = mixed.reshape(rows, heads * HD).astype(BF16)
        branch = dot(mixed, wo)
        r1 = inv_rms(branch)
        middle = x + branch * r1 * g_attn_post
        r2 = inv_rms(middle)
        h2 = (middle * r2 * g_ffn_in).astype(BF16)
        at.append((query_raw, rq, query, keys, values, valid, log_total, mixed, branch, r1, middle, r2, h2))

    ff = []
    for m in range(mb):
        h2 = at[m][-1]
        gate = dot(h2, w_gate)
        up = dot(h2, w_up)
        hidden = (jax.nn.gelu(gate, approximate=True) * up).astype(BF16)
        part = dot(hidden, w_down).astype(BF16)
        ff.append((gate.astype(BF16), up.astype(BF16), hidden, part, swap_y(part)))

    outputs = []
    bw = []
    gain_post = 0.0
    for m in range(mb):
        gate, up, hidden, part, got = ff[m]
        middle = at[m][10]
        ffn = part.astype(F32) + got.astype(F32)
        r3 = inv_rms(ffn)
        cot = cotangent[m].astype(F32)
        outputs.append((middle + ffn * r3 * g_ffn_post).astype(BF16))
        d_ffn = pull_v(ffn, r3, g_ffn_post, cot).astype(BF16)
        gain_post = gain_post + jnp.sum(cot * ffn * r3, axis=0)
        d_hidden = dot(d_ffn, w_down, 1, 1)
        act, pull = jax.vjp(lambda v: jax.nn.gelu(v, approximate=True), gate.astype(F32))
        d_up = (d_hidden * act).astype(BF16)
        (d_gate,) = pull(d_hidden * up.astype(F32))
        d_gate = d_gate.astype(BF16)
        dh2 = (dot(d_gate, w_gate, 1, 1) + dot(d_up, w_up, 1, 1)).astype(BF16)
        bw.append((d_ffn, d_gate, d_up, dh2, swap_y(dh2), cot))

    def rows_of(parts):
        return jnp.concatenate(parts, 0)

    grad_down = scatter_sum(halves_first(rows_of([b[0] for b in bw])), rows_of([f[2] for f in ff]))
    h2_t = halves_first(rows_of([a[-1] for a in at]))
    grad_gate = scatter_sum(h2_t, rows_of([b[1] for b in bw]))
    grad_up = scatter_sum(h2_t, rows_of([b[2] for b in bw]))

    gain_ffn_in = gain_attn_post = gain_query = 0.0
    d_branches = []
    dqs = []
    back = []
    for m in range(mb):
        query_raw, rq, query, keys, values, valid, log_total, mixed, branch, r1, middle, r2, h2 = at[m]
        dh2_sum = bw[m][3].astype(F32) + bw[m][4].astype(F32)
        d_middle = bw[m][5] + pull_v(middle, r2, g_ffn_in, dh2_sum)
        gain_ffn_in = gain_ffn_in + jnp.sum(dh2_sum * middle * r2, axis=0)
        gain_attn_post = gain_attn_post + jnp.sum(d_middle * branch * r1, axis=0)
        d_branch = pull_v(branch, r1, g_attn_post, d_middle).astype(BF16)
        d_mixed = dot(d_branch, wo, 1, 1).astype(BF16).reshape(rows, heads, HD)
        scores = jnp.einsum("qhd,kd->hqk", query, keys, preferred_element_type=F32)
        scores = jnp.where(valid[None], scores, NEGATIVE)
        probs = jnp.exp(scores - log_total)
        d_probs = jnp.einsum("qhd,kd->hqk", d_mixed, values, preferred_element_type=F32)
        row_dot = jnp.sum(probs * d_probs, axis=-1, keepdims=True)
        d_scores = (probs * (d_probs - row_dot)).astype(BF16)
        d_query = jnp.einsum("hqk,kd->qhd", d_scores, keys, preferred_element_type=F32)
        d_key = jnp.einsum("hqk,qhd->kd", d_scores, query, preferred_element_type=F32)
        d_value = jnp.einsum("hqk,qhd->kd", probs.astype(BF16), d_mixed, preferred_element_type=F32)
        sent = shift_dp((d_key[:rows].astype(BF16), d_value[:rows].astype(BF16)), -1)
        e_q = rotate(d_query * scale, cos_h, -sin_h)
        gain_query = gain_query + jnp.sum(e_q * query_raw * rq, axis=(0, 1))
        dqr = pull_v(query_raw, rq, g_query, e_q).astype(BF16).reshape(rows, heads * HD)
        d_branches.append(d_branch)
        dqs.append(dqr)
        back.append((d_middle, d_key[rows:], d_value[rows:], sent))

    gain_key = gain_in = 0.0
    kvs = []
    grad_inputs = []
    for m in range(mb):
        x, r0, h1, key_raw, rk, key, value, near = fw[m]
        d_middle, d_key, d_value, sent = back[m]
        e_k = rotate(d_key + sent[0].astype(F32), cosine, -sine)
        gain_key = gain_key + jnp.sum(e_k * key_raw * rk, axis=0)
        dkr = pull_v(key_raw, rk, g_key, e_k).astype(BF16)
        dvr = (d_value + sent[1].astype(F32)).astype(BF16)
        d_h1 = dot(dqs[m], wq, 1, 1) + dot(dkr, w_key, 1, 1) + dot(dvr, w_value, 1, 1)
        gain_in = gain_in + jnp.sum(d_h1 * x * r0, axis=0)
        grad_inputs.append(d_middle + pull_v(x, r0, g_attn_in, d_h1))
        kvs.append(jnp.concatenate([dkr, dvr], 1))

    def own(a):
        return lax.dynamic_slice_in_dim(a, y * heads_own * HD, heads_own * HD, 1)

    grad_out = scatter_sum(halves_first(rows_of(d_branches)), own(rows_of([a[7] for a in at])))
    h1_t = halves_first(rows_of([f[2] for f in fw]))
    grad_qkv = scatter_sum(
        h1_t, jnp.concatenate([own(rows_of(dqs)), rows_of(kvs)], 1)
    )
    qw = heads_own * HD
    n = lax.axis_size("dp")
    wide = jnp.stack([gain_in, gain_post, gain_ffn_in, gain_attn_post])
    wide = wide.reshape(4, n, -1).transpose(1, 0, 2).reshape(n, -1)
    small = jnp.stack([gain_query, gain_key]).reshape(2, n, -1).transpose(1, 0, 2).reshape(n, -1)
    gains = lax.psum(jnp.concatenate([wide, small], 1), "dp")
    gains = pick(gains, dp)
    rps = width // n
    hps = HD // n
    g_in, g_post, g_ffn, g_attn = [gains[i * rps : (i + 1) * rps] for i in range(4)]
    gq = gains[4 * rps : 4 * rps + hps]
    gk = gains[4 * rps + hps :]
    return (
        jnp.stack(outputs),
        jnp.stack(grad_inputs),
        g_in,
        grad_qkv[:, :qw],
        grad_qkv[:, qw : qw + HD],
        grad_qkv[:, qw + HD :],
        gq,
        gk,
        grad_out.T,
        g_attn,
        g_ffn,
        grad_gate,
        grad_up,
        grad_down.T,
        g_post,
    )


def solution(mesh):
    rows = P(None, "dp", None)
    in_specs = (
        rows,
        P(None, "dp"),
        P(),
        P(None, "tensor"),
        P(),
        P(),
        P(),
        P(),
        P("tensor", None),
        P(),
        P(),
        P(None, "tensor"),
        P(None, "tensor"),
        P("tensor", None),
        P(),
        rows,
    )
    out_specs = (
        rows,
        rows,
        P("dp"),
        P("dp", "tensor"),
        P("dp", None),
        P("dp", None),
        P("dp"),
        P("dp"),
        P("tensor", "dp"),
        P("dp"),
        P("dp"),
        P("dp", "tensor"),
        P("dp", "tensor"),
        P("tensor", "dp"),
        P("dp"),
    )
    return jax.shard_map(shards, mesh=mesh, in_specs=in_specs, out_specs=out_specs, check_vma=False)
```

time: 1660 us -> 755 us (0.45)
  waiting for transfers between devices: 1140 us -> 197 us
  other arithmetic: 87 us -> 114 us
  starting transfers between devices: 22 us -> 45.1 us
  blocking collectives: 81.8 us -> 65.1 us
    unnamed x10 -> x0, waiting for transfers between devices: 529 us -> none
    psum x10 -> x0, waiting for transfers between devices: 442 us -> none  [the longest x2 137 us: micro_step(): lax.psum(jnp.dot(hidden_low, w_down, preferred_element_type=jnp.float32),...]
    ppermute x8 -> x36, waiting for transfers between devices: 0.02 us -> 197 us  [the longest x22 178 us: swap_dp(): return lax.ppermute(v, 'dp', [(i, i ^ 1 << bit) for i in range(n)])]
    reduce_scatter x4 -> x0, waiting for transfers between devices: 167 us -> none  [the longest x1 66.7 us: shards(): lax.psum_scatter(totals[1], 'dp', scatter_dimension=0, tiled=True)]
    unnamed x1 -> x0, blocking collectives: 61.3 us -> none
    psum x4 -> x1, blocking collectives: 20.5 us -> 65.1 us  [shards(): gains = lax.psum(jnp.concatenate([wide, small], 1), 'dp')]
    while x406 -> x0, local copies, waits for them, and re-layouts: 42.7 us -> none
    transpose x0 -> x8, local copies, waits for them, and re-layouts: none -> 26.2 us  [the longest x4 15.3 us: halves_first(): t = a.T.reshape((2,) * count + (a.shape[1] // n, a.shape[0]))]
  transfers between devices with their start and end apart: 25 -> 36, of which waited for: 16 -> 13; matrix products, arithmetic and copies ran while one was open for 10% -> 43% of each run, Pallas kernels for 0% -> 0%
where the time goes in v1:
time: 755 us; the launch traced here: 748 us
  matrix products  256 us (34%)
  waiting for transfers between devices  197 us (26%)
  other arithmetic  114 us (15%)
  local copies, waits for them, and re-layouts  66.2 us (9%)
  blocking collectives  65.1 us (9%)
  starting transfers between devices  45.1 us (6%)
    dot_general x38, matrix products, dot(): lax.dot_general(a, b, (((ca,), (cb,)), ((), ())), preferred_element_type=...  211 us
    ppermute x22, waiting for transfers between devices, swap_dp(): return lax.ppermute(v, 'dp', [(i, i ^ 1 << bit) for i in range(n)])  178 us
    psum x1, blocking collectives, shards(): gains = lax.psum(jnp.concatenate([wide, small], 1), 'dp')  65.1 us
    ppermute x22, starting transfers between devices, swap_dp(): return lax.ppermute(v, 'dp', [(i, i ^ 1 << bit) for i in range(n)])  20.7 us
    ppermute x8, starting transfers between devices, shift_dp(): return lax.ppermute(v, 'dp', [(i, i + steps) for i in range(first, last)])  17.4 us
    ppermute x6, waiting for transfers between devices, swap_y(): return lax.ppermute(v, 'tensor', [(0, 1), (1, 0)])  17 us
    unnamed x338, local copies, waits for them, and re-layouts  16.8 us
    transpose x4, local copies, waits for them, and re-layouts, halves_first(): t = a.T.reshape((2,) * count + (a.shape[1] // n, a.shape[0]))  15.3 us
  transfers between devices with their start and end apart: 36, of which 13 were waited for; matrix products, arithmetic and copies ran while one was open for 43% of the time, Pallas kernels for 0%

profile of v1, /device:TPU:0, one launch (start us, length us, event | category | flops | bytes accessed | tf_op | source)
XLA Modules:
  0.0 748.4 jit_solution(8692873052452501152)
XLA Ops:
  48.0 10.9 %maximum_select_fusion = bf16[1152,1024]{1,0:T(8,128)(2,1)} fusion(bf16[576,512]{1,0:T(8,128)(2,1)S(1)} %get-tuple-element.78, bf16[576,512]{1,0:T(8,128)(2,1)S(1)} %get-tuple-element.77, bf16[1152,512]{1,0:T(8,128)(2,1)S(1)} %copy-done.45, pred[]{:T(512)S(6)} %eq.5), kind=kLoop, calls=%fused_computation.161 | loop fusion | flops 15335424 | bytes 4718593 | tf_op jit(solution)/shard_map/jit(_where)/select_n | solution.py:131
  71.9 7.6 %maximum_select_fusion.1 = bf16[1024,1152]{1,0:T(8,128)(2,1)S(1)} fusion(bf16[256,1152]{1,0:T(8,128)(2,1)S(1)} %get-tuple-element.76, bf16[256,1152]{1,0:T(8,128)(2,1)S(1)} %get-tuple-element.75, bf16[512,1152]{1,0:T(8,128)(2,1)S(1)} %copy-done.46, pred[]{:T(512)S(6)} %eq.5), kind=kLoop, calls=%fused_computation.162 | loop fusion | flops 15335424 | bytes 4718593 | tf_op jit(solution)/shard_map/jit(_where)/select_n | solution.py:136
  109.0 6.9 fusion.268
  115.8 11.9 %fusion.24 = (bf16[512,3456]{1,0:T(8,128)(2,1)}, bf16[512,3456]{1,0:T(8,128)(2,1)}) fusion(f32[512,3456]{1,0:T(8,128)} %fusion.268, bf16[512,1152]{1,0:T(8,128)(2,1)S(1)} %get-tuple-element.107, bf16[1152,3456]{1,0:T(8,128)(2,1)} %param.28), kind=kOutput, calls=%fused_computation.49 | convolution fusion | flops 4096327680 | bytes 23298048 | tf_op jit(solution)/shard_map/dot_general | solution.py:17
  127.8 7.9 %convolution_convert_fusion.4 = bf16[512,1152]{1,0:T(8,128)(2,1)} fusion(bf16[512,3456]{1,0:T(8,128)(2,1)} %get-tuple-element.168, bf16[3456,1152]{1,0:T(8,128)(2,1)S(1)} %bitcast.523), kind=kOutput, calls=%fused_computation.106 | convolution fusion | flops 4077453312 | bytes 12681216 | tf_op jit(solution)/shard_map/dot_general | solution.py:17
  137.2 6.8 fusion.269
  144.0 11.2 %fusion.33 = (bf16[512,3456]{1,0:T(8,128)(2,1)S(1)}, bf16[512,3456]{1,0:T(8,128)(2,1)}) fusion(f32[512,3456]{1,0:T(8,128)} %fusion.269, bf16[512,1152]{1,0:T(8,128)(2,1)S(1)} %get-tuple-element.108, bf16[1152,3456]{1,0:T(8,128)(2,1)} %param.28), kind=kOutput, calls=%fused_computation.58 | convolution fusion | flops 4096327680 | bytes 23298048 | tf_op jit(solution)/shard_map/dot_general | solution.py:17
  155.2 6.0 convolution_convert_fusion.3
  200.1 15.6 %fusion.47 = (bf16[512,3456]{1,0:T(8,128)(2,1)}, bf16[512,3456]{1,0:T(8,128)(2,1)}) fusion(f32[512,3456]{1,0:T(8,128)} %fusion.269, bf16[512,3456]{1,0:T(8,128)(2,1)S(1)} %copy-done.152, bf16[512,1152]{1,0:T(8,128)(2,1)S(1)} %get-tuple-element.70, bf16[3456,1152]{1,0:T(8,128)(2,1)} %param.29), kind=kOutput, calls=%fused_computation.72 | convolution fusion | flops 4124639232 | bytes 26836992 | tf_op jit(solution)/shard_map/dot_general | solution.py:17
  218.6 15.4 %fusion.40 = (bf16[512,3456]{1,0:T(8,128)(2,1)}, bf16[512,3456]{1,0:T(8,128)(2,1)}) fusion(f32[512,3456]{1,0:T(8,128)} %fusion.268, bf16[512,3456]{1,0:T(8,128)(2,1)S(1)} %copy-done.151, bf16[512,1152]{1,0:T(8,128)(2,1)S(1)} %get-tuple-element.63, bf16[3456,1152]{1,0:T(8,128)(2,1)} %param.29), kind=kOutput, calls=%fused_computation.65 | convolution fusion | flops 4124639232 | bytes 26836992 | tf_op jit(solution)/shard_map/dot_general | solution.py:17
  234.0 9.4 %fusion.270 = f32[512,1152]{1,0:T(8,128)S(1)} fusion(bf16[512,3456]{1,0:T(8,128)(2,1)} %get-tuple-element.52, bf16[1152,3456]{1,0:T(8,128)(2,1)} %param.27), kind=kOutput, calls=%fused_computation.502 | convolution fusion | flops 4076863488 | bytes 13860864 | tf_op jit(solution)/shard_map/dot_general | solution.py:17
  243.4 9.3 %fusion.56 = bf16[512,1152]{1,0:T(8,128)(2,1)} fusion(f32[512,1152]{1,0:T(8,128)S(1)} %fusion.270, bf16[512,3456]{1,0:T(8,128)(2,1)S(1)} %copy-done.155, bf16[1152,3456]{1,0:T(8,128)(2,1)} %param.28), kind=kOutput, calls=%fused_computation.103 | convolution fusion | flops 4078043136 | bytes 15040512 | tf_op jit(solution)/shard_map/dot_general | solution.py:17
  261.1 9.0 %fusion.272 = f32[512,1152]{1,0:T(8,128)} fusion(bf16[512,3456]{1,0:T(8,128)(2,1)S(1)} %copy-done.157, bf16[1152,3456]{1,0:T(8,128)(2,1)} %param.27), kind=kOutput, calls=%fused_computation.504 | convolution fusion | flops 4076863488 | bytes 13860864 | tf_op jit(solution)/shard_map/dot_general | solution.py:17
  270.1 8.6 %convolution_convert_fusion.2 = bf16[576,3456]{1,0:T(8,128)(2,1)} fusion(bf16[512,3456]{1,0:T(8,128)(2,1)S(1)} %copy-done.157, bf16[512,3456]{1,0:T(8,128)(2,1)} %get-tuple-element.52, bf16[2,576,1024]{2,1,0:T(8,128)(2,1)S(1)} %bitcast.491, s32[]{:T(128)S(6)} %select_n.117), kind=kOutput, calls=%fused_computation.78 | convolution fusion | flops 4093009920 | bytes 12238852 | tf_op jit(solution)/shard_map/dot_general | solution.py:17
  278.7 6.4 convolution_convert_fusion.1
  285.2 8.8 %fusion.57 = bf16[512,1152]{1,0:T(8,128)(2,1)} fusion(f32[512,1152]{1,0:T(8,128)} %fusion.272, bf16[512,3456]{1,0:T(8,128)(2,1)} %get-tuple-element.53, bf16[1152,3456]{1,0:T(8,128)(2,1)S(1)} %bitcast.527), kind=kOutput, calls=%fused_computation.104 | convolution fusion | flops 4078043136 | bytes 15040512 | tf_op jit(solution)/shard_map/dot_general | solution.py:17
  294.5 6.2 convolution_convert_fusion
  307.6 13.5 %collective-permute-done.13 = bf16[512,1152]{1,0:T(8,128)(2,1)} collective-permute-done((bf16[512,1152]{1,0:T(8,128)(2,1)}, bf16[512,1152]{1,0:T(8,128)(2,1)}, u32[]{:S(2)}, u32[]{:S(2)}) %collective-permute-start.13) | collective-permute-done | bytes 1179680 | tf_op jit(solution)/shard_map/ppermute | solution.py:43
  341.1 6.6 convolution_bitcast_fusion.2
  347.7 6.7 convolution_bitcast_fusion
  415.0 8.1 %convolution_convert_fusion.5 = bf16[576,1024]{1,0:T(8,128)(2,1)} fusion(bf16[2,576,1024]{2,1,0:T(8,128)(2,1)S(1)} %bitcast.497, s32[]{:T(128)S(6)} %select_n.117, bf16[512,256]{0,1:T(8,128)(2,1)S(1)} %fusion.170, bf16[512,256]{0,1:T(8,128)(2,1)S(1)} %get-tuple-element.139, bf16[512,256]{0,1:T(8,128)(2,1)S(1)} %fusion.171, ...), kind=kOutput, calls=%fused_computation.233 | convolution fusion | flops 1219035136 | bytes 4456452 | tf_op jit(solution)/shard_map/dot_general | solution.py:17
  446.9 8.2 %add_convert_fusion.3 = bf16[576,1024]{1,0:T(8,128)(2,1)S(1)} fusion(bf16[576,1024]{1,0:T(8,128)(2,1)} %collective-permute-done.16, bf16[2,576,1024]{2,1,0:T(8,128)(2,1)S(1)} %bitcast.498, s32[]{:T(128)S(6)} %select_n.116, bf16[512,256]{0,1:T(8,128)(2,1)S(1)} %copy-done.72, bf16[512,256]{0,1:T(8,128)(2,1)S(1)} %get-tuple-element.139, ...), kind=kOutput, calls=%fused_computation.168 | convolution fusion | flops 1220214784 | bytes 5636100 | tf_op jit(solution)/shard_map/dot_general | solution.py:17
  456.4 65.1 %psum.7 = f32[16,320]{1,0:T(8,128)S(1)} all-reduce(f32[16,320]{1,0:T(8,128)S(1)} %pad_maximum_fusion.23), channel_id=1, replica_groups=mesh['dp'=16,'tensor'=2] {'dp'}, use_global_device_ids=true, to_apply=%region_42.43 | all-reduce | flops 5120 | bytes 40960 | tf_op jit(solution)/shard_map/psum | solution.py:279
  543.3 7.7 %add_convert_fusion.2 = bf16[576,3456]{1,0:T(8,128)(2,1)S(1)} fusion(bf16[576,3456]{1,0:T(8,128)(2,1)} %collective-permute-done.24, bf16[512,3456]{1,0:T(8,128)(2,1)S(1)} %copy-done.158, bf16[512,3456]{1,0:T(8,128)(2,1)} %get-tuple-element.52, bf16[2,576,1024]{2,1,0:T(8,128)(2,1)S(1)} %bitcast.493, s32[]{:T(128)S(6)} %select_n.116), kind=kOutput, calls=%fused_computation.32 | convolution fusion | flops 4096991232 | bytes 16220164 | tf_op jit(solution)/shard_map/dot_general | solution.py:17
  552.9 7.7 %add_convert_fusion.1 = bf16[576,3456]{1,0:T(8,128)(2,1)S(1)} fusion(bf16[576,3456]{1,0:T(8,128)(2,1)} %collective-permute-done.28, bf16[512,3456]{1,0:T(8,128)(2,1)S(1)} %copy-done.154, bf16[512,3456]{1,0:T(8,128)(2,1)} %get-tuple-element.51, bf16[2,576,1024]{2,1,0:T(8,128)(2,1)S(1)} %bitcast.494, s32[]{:T(128)S(6)} %select_n.116), kind=kOutput, calls=%fused_computation.31 | convolution fusion | flops 4096991232 | bytes 16220164 | tf_op jit(solution)/shard_map/dot_general | solution.py:17
  563.0 8.6 %add_convert_fusion = bf16[576,3456]{1,0:T(8,128)(2,1)S(1)} fusion(bf16[576,3456]{1,0:T(8,128)(2,1)} %collective-permute-done.32, bf16[512,3456]{1,0:T(8,128)(2,1)} %copy-done.149, bf16[512,3456]{1,0:T(8,128)(2,1)} %get-tuple-element.168, bf16[2,576,1024]{2,1,0:T(8,128)(2,1)S(1)} %bitcast.496, s32[]{:T(128)S(6)} %select_n.116), kind=kOutput, calls=%fused_computation.30 | convolution fusion | flops 4096991232 | bytes 16220164 | tf_op jit(solution)/shard_map/dot_general | solution.py:17
  572.9 24.5 %collective-permute-done.25 = bf16[288,3456]{1,0:T(8,128)(2,1)S(1)} collective-permute-done((bf16[288,3456]{1,0:T(8,128)(2,1)S(1)}, bf16[288,3456]{1,0:T(8,128)(2,1)S(1)}, u32[]{:S(2)}, u32[]{:S(2)}) %collective-permute-start.25) | collective-permute-done | bytes 1990688 | tf_op jit(solution)/shard_map/ppermute | solution.py:48
  598.2 41.9 %collective-permute-done.29 = bf16[288,3456]{1,0:T(8,128)(2,1)S(1)} collective-permute-done((bf16[288,3456]{1,0:T(8,128)(2,1)}, bf16[288,3456]{1,0:T(8,128)(2,1)S(1)}, u32[]{:S(2)}, u32[]{:S(2)}) %collective-permute-start.29) | collective-permute-done | bytes 1990688 | tf_op jit(solution)/shard_map/ppermute | solution.py:48
  640.8 38.0 %collective-permute-done.33 = bf16[288,3456]{1,0:T(8,128)(2,1)S(1)} collective-permute-done((bf16[288,3456]{1,0:T(8,128)(2,1)S(1)}, bf16[288,3456]{1,0:T(8,128)(2,1)S(1)}, u32[]{:S(2)}, u32[]{:S(2)}) %collective-permute-start.33) | collective-permute-done | bytes 1990688 | tf_op jit(solution)/shard_map/ppermute | solution.py:48
  684.3 37.1 %collective-permute-done.34 = bf16[144,3456]{1,0:T(8,128)(2,1)S(1)} collective-permute-done((bf16[144,3456]{1,0:T(8,128)(2,1)S(1)}, bf16[144,3456]{1,0:T(8,128)(2,1)S(1)}, u32[]{:S(2)}, u32[]{:S(2)}) %collective-permute-start.34) | collective-permute-done | bytes 995360 | tf_op jit(solution)/shard_map/ppermute | solution.py:48
  723.5 13.6 %collective-permute-done.31 = bf16[72,3456]{1,0:T(8,128)(2,1)S(1)} collective-permute-done((bf16[72,3456]{1,0:T(8,128)(2,1)S(1)}, bf16[72,3456]{1,0:T(8,128)(2,1)S(1)}, u32[]{:S(2)}, u32[]{:S(2)}) %collective-permute-start.31) | collective-permute-done | bytes 497696 | tf_op jit(solution)/shard_map/ppermute | solution.py:48
  738.1 9.1 %collective-permute-done.35 = bf16[72,3456]{1,0:T(8,128)(2,1)S(1)} collective-permute-done((bf16[72,3456]{1,0:T(8,128)(2,1)S(1)}, bf16[72,3456]{1,0:T(8,128)(2,1)S(1)}, u32[]{:S(2)}, u32[]{:S(2)}) %collective-permute-start.35) | collective-permute-done | bytes 497696 | tf_op jit(solution)/shard_map/ppermute | solution.py:48
  (579 shorter events, 289.7 us)
Async XLA Ops:
  2.8 34.7 %collective-permute-start.2 = (bf16[576,512]{1,0:T(8,128)(2,1)}, bf16[576,512]{1,0:T(8,128)(2,1)}, u32[]{:S(2)}, u32[]{:S(2)}) collective-permute-start(bf16[576,512]{1,0:T(8,128)(2,1)} %dynamic-slice_bitcast_fusion.8), channel_id=1, source_target_pairs={{0,1},{1,0},{2,3},{3,2},{4,5},{5,4},{6,7},{7,6},{8,9},{9,8},{10,11... | collective-permute-start | bytes 1769480 | tf_op jit(solution)/shard_map/ppermute | solution.py:43
  7.7 35.3 %collective-permute-start.4 = (bf16[256,1152]{1,0:T(8,128)(2,1)}, bf16[256,1152]{1,0:T(8,128)(2,1)}, u32[]{:S(2)}, u32[]{:S(2)}) collective-permute-start(bf16[256,1152]{1,0:T(8,128)(2,1)} %dynamic-slice_bitcast_fusion.7), channel_id=1, source_target_pairs={{0,1},{1,0},{2,3},{3,2},{4,5},{5,4},{6,7},{7,6},{8,9},{9,8},{10,11... | collective-permute-start | bytes 1769480 | tf_op jit(solution)/shard_map/ppermute | solution.py:43
  10.7 87.7 %collective-permute-start.7 = (bf16[512,256]{1,0:T(8,128)(2,1)}, bf16[512,256]{1,0:T(8,128)(2,1)}, u32[]{:S(2)}, u32[]{:S(2)}) collective-permute-start(bf16[512,256]{1,0:T(8,128)(2,1)} %convolution_convert_fusion.11), channel_id=1, source_target_pairs={{0,2},{2,4},{4,6},{6,8},{8,10},{10,12},{12,14},{14,16},{16,18},{18... | collective-permute-start | bytes 786440 | tf_op jit(solution)/shard_map/ppermute | solution.py:54
  14.1 72.1 %collective-permute-start = (bf16[512,256]{1,0:T(8,128)(2,1)}, bf16[512,256]{1,0:T(8,128)(2,1)}, u32[]{:S(2)}, u32[]{:S(2)}) collective-permute-start(bf16[512,256]{1,0:T(8,128)(2,1)} %convolution_convert_fusion.12), channel_id=1, source_target_pairs={{0,2},{2,4},{4,6},{6,8},{8,10},{10,12},{12,14},{14,16},{16,18},{18... | collective-permute-start | bytes 786440 | tf_op jit(solution)/shard_map/ppermute | solution.py:54
  32.1 60.9 %collective-permute-start.8 = (bf16[512,256]{0,1:T(8,128)(2,1)}, bf16[512,256]{0,1:T(8,128)(2,1)}, u32[]{:S(2)}, u32[]{:S(2)}) collective-permute-start(bf16[512,256]{0,1:T(8,128)(2,1)} %pad_maximum_fusion.22), channel_id=1, source_target_pairs={{0,2},{2,4},{4,6},{6,8},{8,10},{10,12},{12,14},{14,16},{16,18},{18... | collective-permute-start | bytes 786440 | tf_op jit(solution)/shard_map/ppermute | solution.py:54
  37.4 8.1 %collective-permute-start.3 = (bf16[576,512]{1,0:T(8,128)(2,1)}, bf16[576,512]{1,0:T(8,128)(2,1)S(1)}, u32[]{:S(2)}, u32[]{:S(2)}) collective-permute-start(bf16[576,512]{1,0:T(8,128)(2,1)} %collective-permute-done.2), channel_id=1, source_target_pairs={{0,2},{2,0},{4,6},{6,4},{8,10},{10,8},{12,14},{14,12},{16,18},{18,... | collective-permute-start | bytes 1769480 | tf_op jit(solution)/shard_map/ppermute | solution.py:48
  42.9 38.7 %collective-permute-start.1 = (bf16[512,256]{0,1:T(8,128)(2,1)}, bf16[512,256]{0,1:T(8,128)(2,1)}, u32[]{:S(2)}, u32[]{:S(2)}) collective-permute-start(bf16[512,256]{0,1:T(8,128)(2,1)} %pad_maximum_fusion.21), channel_id=1, source_target_pairs={{0,2},{2,4},{4,6},{6,8},{8,10},{10,12},{12,14},{14,16},{16,18},{18... | collective-permute-start | bytes 786440 | tf_op jit(solution)/shard_map/ppermute | solution.py:54
  45.6 24.1 %collective-permute-start.5 = (bf16[256,1152]{1,0:T(8,128)(2,1)}, bf16[256,1152]{1,0:T(8,128)(2,1)}, u32[]{:S(2)}, u32[]{:S(2)}) collective-permute-start(bf16[256,1152]{1,0:T(8,128)(2,1)} %collective-permute-done.4), channel_id=1, source_target_pairs={{0,2},{2,0},{4,6},{6,4},{8,10},{10,8},{12,14},{14,12},{16,18},{18,... | collective-permute-start | bytes 1769480 | tf_op jit(solution)/shard_map/ppermute | solution.py:48
  135.7 47.8 %collective-permute-start.6 = (bf16[512,1152]{1,0:T(8,128)(2,1)}, bf16[512,1152]{1,0:T(8,128)(2,1)}, u32[]{:S(2)}, u32[]{:S(2)}) collective-permute-start(bf16[512,1152]{1,0:T(8,128)(2,1)} %convolution_convert_fusion.4), channel_id=1, source_target_pairs={{0,1},{1,0},{2,3},{3,2},{4,5},{5,4},{6,7},{7,6},{8,9},{9,8},{10,11... | collective-permute-start | bytes 3538952 | tf_op jit(solution)/shard_map/ppermute | solution.py:43
  161.2 28.0 %collective-permute-start.9 = (bf16[512,1152]{1,0:T(8,128)(2,1)}, bf16[512,1152]{1,0:T(8,128)(2,1)}, u32[]{:S(2)}, u32[]{:S(2)}) collective-permute-start(bf16[512,1152]{1,0:T(8,128)(2,1)} %convolution_convert_fusion.3), channel_id=1, source_target_pairs={{0,1},{1,0},{2,3},{3,2},{4,5},{5,4},{6,7},{7,6},{8,9},{9,8},{10,11... | collective-permute-start | bytes 3538952 | tf_op jit(solution)/shard_map/ppermute | solution.py:43
  252.6 52.3 %collective-permute-start.10 = (bf16[512,1152]{1,0:T(8,128)(2,1)}, bf16[512,1152]{1,0:T(8,128)(2,1)}, u32[]{:S(2)}, u32[]{:S(2)}) collective-permute-start(bf16[512,1152]{1,0:T(8,128)(2,1)} %fusion.56), channel_id=1, source_target_pairs={{0,1},{1,0},{2,3},{3,2},{4,5},{5,4},{6,7},{7,6},{8,9},{9,8},{10,11... | collective-permute-start | bytes 3538952 | tf_op jit(solution)/shard_map/ppermute | solution.py:43
  294.0 27.1 %collective-permute-start.13 = (bf16[512,1152]{1,0:T(8,128)(2,1)}, bf16[512,1152]{1,0:T(8,128)(2,1)}, u32[]{:S(2)}, u32[]{:S(2)}) collective-permute-start(bf16[512,1152]{1,0:T(8,128)(2,1)} %fusion.57), channel_id=1, source_target_pairs={{0,1},{1,0},{2,3},{3,2},{4,5},{5,4},{6,7},{7,6},{8,9},{9,8},{10,11... | collective-permute-start | bytes 3538952 | tf_op jit(solution)/shard_map/ppermute | solution.py:43
  300.9 242.4 %collective-permute-start.24 = (bf16[576,3456]{1,0:T(8,128)(2,1)}, bf16[576,3456]{1,0:T(8,128)(2,1)}, u32[]{:S(2)}, u32[]{:S(2)}) collective-permute-start(bf16[576,3456]{1,0:T(8,128)(2,1)} %convolution_convert_fusion.2), channel_id=1, source_target_pairs={{0,2},{2,0},{4,6},{6,4},{8,10},{10,8},{12,14},{14,12},{16,18},{18,... | collective-permute-start | bytes 11943944 | tf_op jit(solution)/shard_map/ppermute | solution.py:48
  300.9 250.2 %collective-permute-start.28 = (bf16[576,3456]{1,0:T(8,128)(2,1)}, bf16[576,3456]{1,0:T(8,128)(2,1)}, u32[]{:S(2)}, u32[]{:S(2)}) collective-permute-start(bf16[576,3456]{1,0:T(8,128)(2,1)} %convolution_convert_fusion.1), channel_id=1, source_target_pairs={{0,2},{2,0},{4,6},{6,4},{8,10},{10,8},{12,14},{14,12},{16,18},{18,... | collective-permute-start | bytes 11943944 | tf_op jit(solution)/shard_map/ppermute | solution.py:48
  301.4 260.9 %collective-permute-start.32 = (bf16[576,3456]{1,0:T(8,128)(2,1)}, bf16[576,3456]{1,0:T(8,128)(2,1)}, u32[]{:S(2)}, u32[]{:S(2)}) collective-permute-start(bf16[576,3456]{1,0:T(8,128)(2,1)} %convolution_convert_fusion), channel_id=1, source_target_pairs={{0,2},{2,0},{4,6},{6,4},{8,10},{10,8},{12,14},{14,12},{16,18},{18,... | collective-permute-start | bytes 11943944 | tf_op jit(solution)/shard_map/ppermute | solution.py:48
  367.2 28.1 %collective-permute-start.14 = (bf16[512,256]{0,1:T(8,128)(2,1)}, bf16[512,256]{0,1:T(8,128)(2,1)S(1)}, u32[]{:S(2)}, u32[]{:S(2)}) collective-permute-start(bf16[512,256]{0,1:T(8,128)(2,1)} %slice.284), channel_id=1, source_target_pairs={{2,0},{4,2},{6,4},{8,6},{10,8},{12,10},{14,12},{16,14},{18,16},{20... | collective-permute-start | bytes 786440 | tf_op jit(solution)/shard_map/ppermute | solution.py:54
  377.2 20.9 %collective-permute-start.11 = (bf16[512,256]{0,1:T(8,128)(2,1)}, bf16[512,256]{0,1:T(8,128)(2,1)S(1)}, u32[]{:S(2)}, u32[]{:S(2)}) collective-permute-start(bf16[512,256]{0,1:T(8,128)(2,1)} %slice.286), channel_id=1, source_target_pairs={{2,0},{4,2},{6,4},{8,6},{10,8},{12,10},{14,12},{16,14},{18,16},{20... | collective-permute-start | bytes 786440 | tf_op jit(solution)/shard_map/ppermute | solution.py:54
  395.2 46.2 %collective-permute-start.20 = (bf16[576,512]{1,0:T(8,128)(2,1)}, bf16[576,512]{1,0:T(8,128)(2,1)}, u32[]{:S(2)}, u32[]{:S(2)}) collective-permute-start(bf16[576,512]{1,0:T(8,128)(2,1)} %convolution_convert_fusion.10), channel_id=1, source_target_pairs={{0,2},{2,0},{4,6},{6,4},{8,10},{10,8},{12,14},{14,12},{16,18},{18,... | collective-permute-start | bytes 1769480 | tf_op jit(solution)/shard_map/ppermute | solution.py:48
  398.2 12.4 %collective-permute-start.12 = (bf16[512,256]{0,1:T(8,128)(2,1)S(1)}, bf16[512,256]{0,1:T(8,128)(2,1)S(1)}, u32[]{:S(2)}, u32[]{:S(2)}) collective-permute-start(bf16[512,256]{0,1:T(8,128)(2,1)S(1)} %slice.285), channel_id=1, source_target_pairs={{2,0},{4,2},{6,4},{8,6},{10,8},{12,10},{14,12},{16,14},{18,16},{20... | collective-permute-start | bytes 786440 | tf_op jit(solution)/shard_map/ppermute | solution.py:54
  423.1 23.8 %collective-permute-start.16 = (bf16[576,1024]{1,0:T(8,128)(2,1)}, bf16[576,1024]{1,0:T(8,128)(2,1)}, u32[]{:S(2)}, u32[]{:S(2)}) collective-permute-start(bf16[576,1024]{1,0:T(8,128)(2,1)} %convolution_convert_fusion.5), channel_id=1, source_target_pairs={{0,2},{2,0},{4,6},{6,4},{8,10},{10,8},{12,14},{14,12},{16,18},{18,... | collective-permute-start | bytes 3538952 | tf_op jit(solution)/shard_map/ppermute | solution.py:48
  444.3 78.5 %collective-permute-start.21 = (bf16[288,512]{1,0:T(8,128)(2,1)}, bf16[288,512]{1,0:T(8,128)(2,1)}, u32[]{:S(2)}, u32[]{:S(2)}) collective-permute-start(bf16[288,512]{1,0:T(8,128)(2,1)} %dynamic-slice_bitcast_fusion.12), channel_id=1, source_target_pairs={{0,4},{2,6},{4,0},{6,2},{8,12},{10,14},{12,8},{14,10},{16,20},{18,... | collective-permute-start | bytes 884744 | tf_op jit(solution)/shard_map/ppermute | solution.py:48
  456.2 67.8 %collective-permute-start.17 = (bf16[288,1024]{1,0:T(8,128)(2,1)S(1)}, bf16[288,1024]{1,0:T(8,128)(2,1)S(1)}, u32[]{:S(2)}, u32[]{:S(2)}) collective-permute-start(bf16[288,1024]{1,0:T(8,128)(2,1)S(1)} %dynamic-slice_bitcast_fusion.6), channel_id=1, source_target_pairs={{0,4},{2,6},{4,0},{6,2},{8,12},{10,14},{12,8},{14,10},{16,20},{18,... | collective-permute-start | bytes 1769480 | tf_op jit(solution)/shard_map/ppermute | solution.py:48
  525.5 8.6 %collective-permute-start.18 = (bf16[144,1024]{1,0:T(8,128)(2,1)S(1)}, bf16[144,1024]{1,0:T(8,128)(2,1)S(1)}, u32[]{:S(2)}, u32[]{:S(2)}) collective-permute-start(bf16[144,1024]{1,0:T(8,128)(2,1)S(1)} %dynamic-slice_bitcast_fusion.13), channel_id=1, source_target_pairs={{0,8},{2,10},{4,12},{6,14},{8,0},{10,2},{12,4},{14,6},{16,24},{18,... | collective-permute-start | bytes 884744 | tf_op jit(solution)/shard_map/ppermute | solution.py:48
  551.1 46.4 %collective-permute-start.25 = (bf16[288,3456]{1,0:T(8,128)(2,1)S(1)}, bf16[288,3456]{1,0:T(8,128)(2,1)S(1)}, u32[]{:S(2)}, u32[]{:S(2)}) collective-permute-start(bf16[288,3456]{1,0:T(8,128)(2,1)S(1)} %dynamic-slice_bitcast_fusion.2), channel_id=1, source_target_pairs={{0,4},{2,6},{4,0},{6,2},{8,12},{10,14},{12,8},{14,10},{16,20},{18,... | collective-permute-start | bytes 5971976 | tf_op jit(solution)/shard_map/ppermute | solution.py:48
  562.0 78.1 %collective-permute-start.29 = (bf16[288,3456]{1,0:T(8,128)(2,1)}, bf16[288,3456]{1,0:T(8,128)(2,1)S(1)}, u32[]{:S(2)}, u32[]{:S(2)}) collective-permute-start(bf16[288,3456]{1,0:T(8,128)(2,1)} %dynamic-slice_bitcast_fusion.1), channel_id=1, source_target_pairs={{0,4},{2,6},{4,0},{6,2},{8,12},{10,14},{12,8},{14,10},{16,20},{18,... | collective-permute-start | bytes 5971976 | tf_op jit(solution)/shard_map/ppermute | solution.py:48
  571.8 107.1 %collective-permute-start.33 = (bf16[288,3456]{1,0:T(8,128)(2,1)S(1)}, bf16[288,3456]{1,0:T(8,128)(2,1)S(1)}, u32[]{:S(2)}, u32[]{:S(2)}) collective-permute-start(bf16[288,3456]{1,0:T(8,128)(2,1)S(1)} %dynamic-slice_bitcast_fusion), channel_id=1, source_target_pairs={{0,4},{2,6},{4,0},{6,2},{8,12},{10,14},{12,8},{14,10},{16,20},{18,... | collective-permute-start | bytes 5971976 | tf_op jit(solution)/shard_map/ppermute | solution.py:48
  598.0 82.3 %collective-permute-start.26 = (bf16[144,3456]{1,0:T(8,128)(2,1)S(1)}, bf16[144,3456]{1,0:T(8,128)(2,1)S(1)}, u32[]{:S(2)}, u32[]{:S(2)}) collective-permute-start(bf16[144,3456]{1,0:T(8,128)(2,1)S(1)} %dynamic-slice_bitcast_fusion.5), channel_id=1, source_target_pairs={{0,8},{2,10},{4,12},{6,14},{8,0},{10,2},{12,4},{14,6},{16,24},{18,... | collective-permute-start | bytes 2985992 | tf_op jit(solution)/shard_map/ppermute | solution.py:48
  640.7 43.2 %collective-permute-start.30 = (bf16[144,3456]{1,0:T(8,128)(2,1)S(1)}, bf16[144,3456]{1,0:T(8,128)(2,1)S(1)}, u32[]{:S(2)}, u32[]{:S(2)}) collective-permute-start(bf16[144,3456]{1,0:T(8,128)(2,1)S(1)} %dynamic-slice_bitcast_fusion.4), channel_id=1, source_target_pairs={{0,8},{2,10},{4,12},{6,14},{8,0},{10,2},{12,4},{14,6},{16,24},{18,... | collective-permute-start | bytes 2985992 | tf_op jit(solution)/shard_map/ppermute | solution.py:48
  679.5 41.9 %collective-permute-start.34 = (bf16[144,3456]{1,0:T(8,128)(2,1)S(1)}, bf16[144,3456]{1,0:T(8,128)(2,1)S(1)}, u32[]{:S(2)}, u32[]{:S(2)}) collective-permute-start(bf16[144,3456]{1,0:T(8,128)(2,1)S(1)} %dynamic-slice_bitcast_fusion.3), channel_id=1, source_target_pairs={{0,8},{2,10},{4,12},{6,14},{8,0},{10,2},{12,4},{14,6},{16,24},{18,... | collective-permute-start | bytes 2985992 | tf_op jit(solution)/shard_map/ppermute | solution.py:48
  680.6 41.8 %collective-permute-start.27 = (bf16[72,3456]{1,0:T(8,128)(2,1)S(1)}, bf16[72,3456]{1,0:T(8,128)(2,1)S(1)}, u32[]{:S(2)}, u32[]{:S(2)}) collective-permute-start(bf16[72,3456]{1,0:T(8,128)(2,1)S(1)} %dynamic-slice_bitcast_fusion.11), channel_id=1, source_target_pairs={{0,16},{2,18},{4,20},{6,22},{8,24},{10,26},{12,28},{14,30},{16,0},... | collective-permute-start | bytes 1493000 | tf_op jit(solution)/shard_map/ppermute | solution.py:48
  684.2 52.9 %collective-permute-start.31 = (bf16[72,3456]{1,0:T(8,128)(2,1)S(1)}, bf16[72,3456]{1,0:T(8,128)(2,1)S(1)}, u32[]{:S(2)}, u32[]{:S(2)}) collective-permute-start(bf16[72,3456]{1,0:T(8,128)(2,1)S(1)} %dynamic-slice_bitcast_fusion.10), channel_id=1, source_target_pairs={{0,16},{2,18},{4,20},{6,22},{8,24},{10,26},{12,28},{14,30},{16,0},... | collective-permute-start | bytes 1493000 | tf_op jit(solution)/shard_map/ppermute | solution.py:48
  721.7 25.5 %collective-permute-start.35 = (bf16[72,3456]{1,0:T(8,128)(2,1)S(1)}, bf16[72,3456]{1,0:T(8,128)(2,1)S(1)}, u32[]{:S(2)}, u32[]{:S(2)}) collective-permute-start(bf16[72,3456]{1,0:T(8,128)(2,1)S(1)} %dynamic-slice_bitcast_fusion.9), channel_id=1, source_target_pairs={{0,16},{2,18},{4,20},{6,22},{8,24},{10,26},{12,28},{14,30},{16,0},... | collective-permute-start | bytes 1493000 | tf_op jit(solution)/shard_map/ppermute | solution.py:48
  (173 other events, 1188.3 us)
